TPU v7x, 512 devices: a whole 4x8x8 slice. The times are simulated.
512 devices in a mesh: seq: 128 (over z, x, y_hi), dp: 4 (over y_lo, core).
Axes of the slice: x: 4, y: 8 (y_hi: 4, y_lo: 2; y = y_hi * 2 + y_lo), z: 8, core: 2. Of those that a mesh axis runs over, the one named last changes fastest.
Arguments:
- q_raw: bfloat16 [4, 16384, 2560], P('dp', 'seq'), may hold values from -40 to 40
- k_raw: bfloat16 [4, 16384, 2560], P('dp', 'seq'), may hold values from -40 to 40
- values: bfloat16 [4, 16384, 2560], P('dp', 'seq'), may hold values from -6 to 6
- d_attn: bfloat16 [4, 16384, 2560], P('dp', 'seq'), may hold values from -180 to 180
- q_gain: float32 [2560], replicated, may hold values from 0.5 to 1.5
- k_gain: float32 [2560], replicated, may hold values from 0.5 to 1.5
- kv_lists: int32 [128, 5], P('seq'), may hold values from -1 to 127, as said below
Outputs:
- d_q_raw: bfloat16 [4, 16384, 2560], P('dp', 'seq')
- d_k_raw: bfloat16 [4, 16384, 2560], P('dp', 'seq')
- d_values: bfloat16 [4, 16384, 2560], P('dp', 'seq')
- d_q_gain: float32 [2560], replicated
- d_k_gain: float32 [2560], replicated
Inputs may be any that keep to these rules, and one draw needn't show every extreme that they name: `kv_lists`: row b serves query block b. Slot 0 holds b; for l below 2, slot 2l+1 holds b - 2^l or -1 and slot 2l+2 holds b + 2^l or -1; a slot is -1 whenever its block would lie outside the video, and any slot other than slot 0 may also be -1 because an earlier pruning step dropped that key block.
All inputs are finite; a program needn't handle non-finite values.
Results may differ from a plain program's by a relative error of at most 0.022.
Values may be sent and summed in bfloat16 or wider, within the bound.
A program may use at most 128 MiB of HBM per device.

v0:
```python
import math

import jax
import jax.numpy as jnp
from jax import lax
from jax.sharding import PartitionSpec as P

HEADS = 20
HEAD_DIM = 128
BLOCK = 128
LEVELS = 2


epsilon = 1e-06


def shifted(block, axis, distance):
    devices = range(lax.axis_size(axis))
    route = [(i - distance, i) for i in devices if i - distance in devices]
    return lax.ppermute(block, axis, route)


def offset_list(levels):
    offsets = [0]
    for stride_exp in range(levels):
        offsets = offsets + [-(2**stride_exp), 2**stride_exp]
    return offsets


def norm_forward(raw_in, gain_vec):
    as_float = raw_in.astype(jnp.float32)
    inv_rms = lax.rsqrt(jnp.mean(as_float * as_float, axis=-1, keepdims=True) + epsilon)
    return (as_float, inv_rms, (as_float * inv_rms * gain_vec).astype(jnp.bfloat16))


def norm_backward(as_float, inv_rms, gain_vec, grad_norm):
    scaled = gain_vec * grad_norm
    inner_mean = jnp.mean(scaled * as_float, axis=-1, keepdims=True)
    grad_raw = inv_rms * scaled - as_float * inv_rms * inv_rms * inv_rms * inner_mean
    gain_term = jnp.sum(grad_norm * as_float * inv_rms, axis=tuple(range(grad_norm.ndim - 1)))
    return (grad_raw.astype(jnp.bfloat16), gain_term)


def heads_first(flat_rows, block_shape):
    return jnp.transpose(flat_rows.reshape(block_shape), (0, 2, 1, 3))


def body(q_raw, k_raw, values, d_attn, q_gain, k_gain, kv_lists):
    videos, tokens, features = q_raw.shape
    blocks = tokens // BLOCK
    block_shape = (videos * blocks, BLOCK, HEADS, HEAD_DIM)
    score_scale = 1.0 / math.sqrt(HEAD_DIM)
    q_float, q_inv, q_norm = norm_forward(q_raw, q_gain)
    k_float, k_inv, k_norm = norm_forward(k_raw, k_gain)
    queries = heads_first(q_norm, block_shape)
    grad_out = heads_first(d_attn, block_shape)
    local_pair = jnp.stack([heads_first(k_norm, block_shape), heads_first(values, block_shape)])
    offsets = offset_list(LEVELS)
    live_mask = jnp.tile(kv_lists >= 0, (videos, 1))
    key_mask = jnp.repeat(live_mask, BLOCK, axis=1)
    fetched = {0: local_pair}
    for offset in offsets[1:]:
        fetched[offset] = shifted(local_pair, "seq", -offset)
    joined = jnp.concatenate([fetched[offset] for offset in offsets], axis=3)
    keys_all = joined[0]
    values_all = joined[1]
    raw_scores = (
        jnp.einsum("rhqd,rhkd->rhqk", queries, keys_all, preferred_element_type=jnp.float32)
        * score_scale
    )
    scores = jnp.where(key_mask[:, None, None, :], raw_scores, -jnp.inf)
    row_top = jnp.max(scores, axis=-1, keepdims=True)
    log_total = row_top + jnp.log(jnp.sum(jnp.exp(scores - row_top), axis=-1, keepdims=True))
    prob_full = jnp.exp(scores - log_total)
    prob_half = prob_full.astype(jnp.bfloat16)
    attn_out = jnp.einsum(
        "rhqk,rhkd->rhqd", prob_half, values_all, preferred_element_type=jnp.float32
    ).astype(jnp.bfloat16)
    delta_rows = jnp.einsum(
        "rhqd,rhqd->rhq", grad_out, attn_out, preferred_element_type=jnp.float32
    )
    grad_prob = jnp.einsum(
        "rhqd,rhkd->rhqk", grad_out, values_all, preferred_element_type=jnp.float32
    )
    grad_score = (prob_full * (grad_prob - delta_rows[..., None])).astype(jnp.bfloat16)
    grad_queries = (
        jnp.einsum("rhqk,rhkd->rhqd", grad_score, keys_all, preferred_element_type=jnp.float32)
        * score_scale
    )
    grad_keys_all = (
        jnp.einsum("rhqk,rhqd->rhkd", grad_score, queries, preferred_element_type=jnp.float32)
        * score_scale
    )
    grad_values_all = jnp.einsum(
        "rhqk,rhqd->rhkd", prob_half, grad_out, preferred_element_type=jnp.float32
    )
    grad_pair = jnp.zeros((2,) + local_pair.shape[1:], jnp.float32)
    for slot_index, offset in enumerate(offsets):
        lower = slot_index * BLOCK
        pair_term = jnp.stack(
            [
                grad_keys_all[:, :, lower : lower + BLOCK],
                grad_values_all[:, :, lower : lower + BLOCK],
            ]
        )
        if offset == 0:
            grad_pair = pair_term
        else:
            returned = shifted(pair_term.astype(jnp.bfloat16), "seq", offset)
            grad_pair = grad_pair + returned.astype(jnp.float32)
    flat_shape = (videos, tokens, features)
    d_q_raw, q_term = norm_backward(
        q_float, q_inv, q_gain, jnp.transpose(grad_queries, (0, 2, 1, 3)).reshape(flat_shape)
    )
    d_k_raw, k_term = norm_backward(
        k_float, k_inv, k_gain, jnp.transpose(grad_pair[0], (0, 2, 1, 3)).reshape(flat_shape)
    )
    d_values = jnp.transpose(grad_pair[1], (0, 2, 1, 3)).reshape(flat_shape).astype(jnp.bfloat16)
    q_sum, k_sum = lax.psum((q_term, k_term), ("seq", "dp"))
    norm_count = math.sqrt(videos * tokens * lax.axis_size("seq") * lax.axis_size("dp"))
    return (d_q_raw, d_k_raw, d_values, q_sum / norm_count, k_sum / norm_count)


def solution(mesh):
    placed = (
        P("dp", "seq", None),
        P("dp", "seq", None),
        P("dp", "seq", None),
        P("dp", "seq", None),
        P(),
        P(),
        P("seq", None),
    )
    return jax.shard_map(
        body,
        mesh=mesh,
        in_specs=placed,
        out_specs=(P("dp", "seq", None), P("dp", "seq", None), P("dp", "seq", None), P(), P()),
        check_vma=False,
    )
```

profile of v0, /device:TPU:1, one launch (start us, length us, event | category | flops | bytes accessed | tf_op | source)
XLA Modules:
  0.0 525.4 jit_solution(11476841133337062048)
XLA Ops:
  0.6 1.5 copy.24
  2.1 0.4 fusion.31
  2.5 1.1 fusion.17
  3.6 0.3 copy.25
  4.0 0.3 copy.26
  4.3 0.0 copy-start.12
  4.3 0.0 copy-start.9
  4.3 0.3 copy.27
  4.6 2.2 pad_maximum_fusion
  6.8 8.5 %collective-permute-start.2 = (bf16[2,1,20,128,128]{4,3,2,1,0:T(8,128)(2,1)}, bf16[2,1,20,128,128]{4,3,2,1,0:T(8,128)(2,1)S(1)}, u32[]{:S(2)}, u32[]{:S(2)}) collective-permute-start(bf16[2,1,20,128,128]{4,3,2,1,0:T(8,128)(2,1)} %get-tuple-element.29), channel_id=1, source_target_pairs={{0,8},{4,12},{8,16},{12,20},{16,24},{20,28},{24,32},{28,36},{32,40... | collective-permute-start | bytes 3932168 | tf_op jit(solution)/shard_map/ppermute | solution.py:20
  15.3 1.3 collective-permute-start.1
  16.6 5.9 %collective-permute-start = (bf16[2,1,20,128,128]{4,3,2,1,0:T(8,128)(2,1)}, bf16[2,1,20,128,128]{4,3,2,1,0:T(8,128)(2,1)}, u32[]{:S(2)}, u32[]{:S(2)}) collective-permute-start(bf16[2,1,20,128,128]{4,3,2,1,0:T(8,128)(2,1)} %get-tuple-element.29), channel_id=1, source_target_pairs={{0,4},{4,8},{8,12},{12,16},{16,20},{20,24},{24,28},{28,32},{32,36}... | collective-permute-start | bytes 3932168 | tf_op jit(solution)/shard_map/ppermute | solution.py:20
  22.6 1.3 collective-permute-start.3
  23.9 0.1 broadcast_bitcast_fusion
  24.0 0.3 copy.23
  24.3 0.0 copy-start.1
  24.3 2.4 copy.29
  26.7 0.4 fusion.27
  27.1 0.4 fusion.22
  27.5 0.0 copy-start.5
  27.5 72.2 %collective-permute-done = bf16[2,1,20,128,128]{4,3,2,1,0:T(8,128)(2,1)} collective-permute-done((bf16[2,1,20,128,128]{4,3,2,1,0:T(8,128)(2,1)}, bf16[2,1,20,128,128]{4,3,2,1,0:T(8,128)(2,1)}, u32[]{:S(2)}, u32[]{:S(2)}) %collective-permute-start) | collective-permute-done | bytes 1310752 | tf_op jit(solution)/shard_map/ppermute | solution.py:20
  99.7 2.8 constant_dynamic-update-slice_fusion.3
  102.5 29.7 %collective-permute-done.1 = bf16[2,1,20,128,128]{4,3,2,1,0:T(8,128)(2,1)} collective-permute-done((bf16[2,1,20,128,128]{4,3,2,1,0:T(8,128)(2,1)}, bf16[2,1,20,128,128]{4,3,2,1,0:T(8,128)(2,1)}, u32[]{:S(2)}, u32[]{:S(2)}) %collective-permute-start.1) | collective-permute-done | bytes 1310752 | tf_op jit(solution)/shard_map/ppermute | solution.py:20
  132.2 2.8 constant_dynamic-update-slice_fusion.2
  135.0 1.3 constant_dynamic-update-slice_fusion.1
  136.4 20.8 %collective-permute-done.3 = bf16[2,1,20,128,128]{4,3,2,1,0:T(8,128)(2,1)} collective-permute-done((bf16[2,1,20,128,128]{4,3,2,1,0:T(8,128)(2,1)}, bf16[2,1,20,128,128]{4,3,2,1,0:T(8,128)(2,1)}, u32[]{:S(2)}, u32[]{:S(2)}) %collective-permute-start.3) | collective-permute-done | bytes 1310752 | tf_op jit(solution)/shard_map/ppermute | solution.py:20
  157.2 2.8 constant_dynamic-update-slice_fusion
  160.0 3.5 fusion.2
  163.5 1.8 exponential_reduce_fusion
  165.4 1.4 copy-done
  166.8 1.9 copy-done.3
  168.7 2.8 fusion.16
  171.5 2.9 copy.42
  174.5 7.8 %fusion.41 = (bf16[1,20,640,128]{2,3,1,0:T(8,128)(2,1)S(1)}, f32[1,20,640,128]{2,3,1,0:T(8,128)}) fusion(bf16[20,128,128]{1,2,0:T(8,128)(2,1)} %bitcast.109, f32[20,128,640]{2,1,0:T(8,128)} %copy-done, f32[20,128]{1,0:T(8,128)S(1)} %log_add_fusion, pred[640]{0:T(1024)(128)(4,1)S(1)} %broadcast_bitcast_fusion), kind=kOutput, calls=%fused_computation.89 | convolution fusion | flops 427622400 | bytes 17050240 | tf_op jit(solution)/shard_map/rhqk,rhqd->rhkd/dot_general | solution.py:94
  182.3 0.2 multiply_reduce_fusion
  182.5 4.1 fusion
  186.7 1.2 fusion.14
  188.0 3.8 fusion.42
  191.7 0.8 fusion.30
  192.5 1.5 slice_bitcast_fusion.22
  194.0 1.2 pad_maximum_fusion.2
  195.2 33.0 %collective-permute-start.5 = (bf16[2,1,20,128,128]{3,4,2,1,0:T(8,128)(2,1)}, bf16[2,1,20,128,128]{3,4,2,1,0:T(8,128)(2,1)S(1)}, u32[]{:S(2)}, u32[]{:S(2)}) collective-permute-start(bf16[2,1,20,128,128]{3,4,2,1,0:T(8,128)(2,1)} %pad_maximum_fusion.2), channel_id=1, source_target_pairs={{0,4},{4,8},{8,12},{12,16},{16,20},{20,24},{24,28},{28,32},{32,36}... | collective-permute-start | bytes 3932168 | tf_op jit(solution)/shard_map/ppermute | solution.py:20
  228.2 1.2 pad_maximum_fusion.3
  229.3 1.3 collective-permute-start.6
  230.6 1.2 pad_maximum_fusion.4
  231.8 11.7 %collective-permute-start.7 = (bf16[2,1,20,128,128]{3,4,2,1,0:T(8,128)(2,1)}, bf16[2,1,20,128,128]{3,4,2,1,0:T(8,128)(2,1)}, u32[]{:S(2)}, u32[]{:S(2)}) collective-permute-start(bf16[2,1,20,128,128]{3,4,2,1,0:T(8,128)(2,1)} %pad_maximum_fusion.4), channel_id=1, source_target_pairs={{0,8},{4,12},{8,16},{12,20},{16,24},{20,28},{24,32},{28,36},{32,40... | collective-permute-start | bytes 3932168 | tf_op jit(solution)/shard_map/ppermute | solution.py:20
  243.5 1.2 pad_maximum_fusion.1
  244.7 1.5 collective-permute-start.4
  246.2 0.4 fusion.26
  246.6 1.1 copy.33
  247.7 2.0 slice_bitcast_fusion.14
  249.7 6.9 %collective-permute-done.5 = bf16[2,1,20,128,128]{3,4,2,1,0:T(8,128)(2,1)S(1)} collective-permute-done((bf16[2,1,20,128,128]{3,4,2,1,0:T(8,128)(2,1)}, bf16[2,1,20,128,128]{3,4,2,1,0:T(8,128)(2,1)S(1)}, u32[]{:S(2)}, u32[]{:S(2)}) %collective-permute-start.5) | collective-permute-done | bytes 1310752 | tf_op jit(solution)/shard_map/ppermute | solution.py:20
  256.6 87.1 %collective-permute-done.6 = bf16[2,1,20,128,128]{3,4,2,1,0:T(8,128)(2,1)} collective-permute-done((bf16[2,1,20,128,128]{3,4,2,1,0:T(8,128)(2,1)}, bf16[2,1,20,128,128]{3,4,2,1,0:T(8,128)(2,1)}, u32[]{:S(2)}, u32[]{:S(2)}) %collective-permute-start.6) | collective-permute-done | bytes 1310752 | tf_op jit(solution)/shard_map/ppermute | solution.py:20
  343.7 32.6 %collective-permute-done.4 = bf16[2,1,20,128,128]{3,4,2,1,0:T(8,128)(2,1)} collective-permute-done((bf16[2,1,20,128,128]{3,4,2,1,0:T(8,128)(2,1)}, bf16[2,1,20,128,128]{3,4,2,1,0:T(8,128)(2,1)}, u32[]{:S(2)}, u32[]{:S(2)}) %collective-permute-start.4) | collective-permute-done | bytes 1310752 | tf_op jit(solution)/shard_map/ppermute | solution.py:20
  376.2 3.2 fusion.9
  379.5 0.1 slice.104
  379.6 0.1 slice.77
  379.7 1.1 copy.35
  380.8 0.8 fusion.34
  381.5 141.1 %all-reduce = (f32[2560]{0:T(1024)S(1)}, f32[2560]{0:T(1024)S(1)}) all-reduce(f32[2560]{0:T(1024)S(1)} %get-tuple-element.17, f32[2560]{0:T(1024)S(1)} %get-tuple-element.15), channel_id=1, replica_groups=mesh['seq'=128,'dp'=4] {'seq','dp'}, use_global_device_ids=true, to_apply=%region_7.8 | all-reduce | flops 5120 | bytes 40960 | tf_op jit(solution)/shard_map/psum | solution.py:119
  522.6 0.6 broadcast_multiply_fusion.1
  523.2 0.4 fusion.21
  523.7 1.1 copy.34
  524.8 0.6 broadcast_multiply_fusion
  (38 shorter events, 0.1 us)
Async XLA Ops:
  0.6 3.3 copy-start.8
  4.3 19.6 %copy-start.12 = (s32[1,5]{1,0:T(1,128)S(1)}, s32[1,5]{1,0:T(1,128)}, u32[]{:S(2)}) copy-start(s32[1,5]{1,0:T(1,128)} %param.13) | copy-start | bytes 64
  4.3 19.7 %copy-start.9 = (bf16[1,128,2560]{2,1,0:T(8,128)(2,1)S(1)}, bf16[1,128,2560]{2,1,0:T(8,128)(2,1)}, u32[]{:S(2)}) copy-start(bf16[1,128,2560]{2,1,0:T(8,128)(2,1)} %param.7) | copy-start | bytes 1966084
  6.8 20.2 %copy-start.10 = (f32[2560]{0:T(1024)S(1)}, f32[2560]{0:T(1024)}, u32[]{:S(2)}) copy-start(f32[2560]{0:T(1024)} %param.11) | copy-start | bytes 30724
  6.8 128.2 %collective-permute-start.2 = (bf16[2,1,20,128,128]{4,3,2,1,0:T(8,128)(2,1)}, bf16[2,1,20,128,128]{4,3,2,1,0:T(8,128)(2,1)S(1)}, u32[]{:S(2)}, u32[]{:S(2)}) collective-permute-start(bf16[2,1,20,128,128]{4,3,2,1,0:T(8,128)(2,1)} %get-tuple-element.29), channel_id=1, source_target_pairs={{0,8},{4,12},{8,16},{12,20},{16,24},{20,28},{24,32},{28,36},{32,40... | collective-permute-start | bytes 3932168 | tf_op jit(solution)/shard_map/ppermute | solution.py:20
  15.3 116.9 %collective-permute-start.1 = (bf16[2,1,20,128,128]{4,3,2,1,0:T(8,128)(2,1)}, bf16[2,1,20,128,128]{4,3,2,1,0:T(8,128)(2,1)}, u32[]{:S(2)}, u32[]{:S(2)}) collective-permute-start(bf16[2,1,20,128,128]{4,3,2,1,0:T(8,128)(2,1)} %get-tuple-element.29), channel_id=1, source_target_pairs={{4,0},{8,4},{12,8},{16,12},{20,16},{24,20},{28,24},{32,28},{36,32}... | collective-permute-start | bytes 3932168 | tf_op jit(solution)/shard_map/ppermute | solution.py:20
  16.6 83.1 %collective-permute-start = (bf16[2,1,20,128,128]{4,3,2,1,0:T(8,128)(2,1)}, bf16[2,1,20,128,128]{4,3,2,1,0:T(8,128)(2,1)}, u32[]{:S(2)}, u32[]{:S(2)}) collective-permute-start(bf16[2,1,20,128,128]{4,3,2,1,0:T(8,128)(2,1)} %get-tuple-element.29), channel_id=1, source_target_pairs={{0,4},{4,8},{8,12},{12,16},{16,20},{20,24},{24,28},{28,32},{32,36}... | collective-permute-start | bytes 3932168 | tf_op jit(solution)/shard_map/ppermute | solution.py:20
  22.6 134.6 %collective-permute-start.3 = (bf16[2,1,20,128,128]{4,3,2,1,0:T(8,128)(2,1)}, bf16[2,1,20,128,128]{4,3,2,1,0:T(8,128)(2,1)}, u32[]{:S(2)}, u32[]{:S(2)}) collective-permute-start(bf16[2,1,20,128,128]{4,3,2,1,0:T(8,128)(2,1)} %get-tuple-element.29), channel_id=1, source_target_pairs={{8,0},{12,4},{16,8},{20,12},{24,16},{28,20},{32,24},{36,28},{40,32... | collective-permute-start | bytes 3932168 | tf_op jit(solution)/shard_map/ppermute | solution.py:20
  24.3 78.2 %copy-start.1 = (bf16[1,128,2560]{1,2,0:T(8,128)(2,1)}, bf16[1,128,2560]{1,2,0:T(8,128)(2,1)S(1)}, u32[]{:S(2)}) copy-start(bf16[1,128,2560]{1,2,0:T(8,128)(2,1)S(1)} %copy.23) | copy-start | bytes 1966084
  27.5 132.5 %copy-start.5 = (bf16[1,128,2560]{1,2,0:T(8,128)(2,1)}, bf16[1,128,2560]{1,2,0:T(8,128)(2,1)S(1)}, u32[]{:S(2)}) copy-start(bf16[1,128,2560]{1,2,0:T(8,128)(2,1)S(1)} %fusion.22) | copy-start | bytes 1966084
  163.5 3.3 copy-start
  163.5 5.2 copy-start.3
  171.5 11.0 %slice-start = ((s8[6553600]{0:T(1024)(128)(4,1)}), s8[2359296]{0:T(1024)(128)(4,1)S(1)}, s32[]{:S(2)}) async-start(s8[6553600]{0:T(1024)(128)(4,1)} %bitcast.103), calls=%async_computation | async-start | bytes 4718592
  174.5 7.8 %copy-start.4 = (bf16[1,128,2560]{1,2,0:T(8,128)(2,1)S(1)}, bf16[1,128,2560]{1,2,0:T(8,128)(2,1)}, u32[]{:S(2)}) copy-start(bf16[1,128,2560]{1,2,0:T(8,128)(2,1)} %copy.29) | copy-start | bytes 1966084
  174.5 7.8 %copy-start.7 = (f32[20,128,128]{1,2,0:T(8,128)S(1)}, f32[20,128,128]{1,2,0:T(8,128)}, u32[]{:S(2)}) copy-start(f32[20,128,128]{1,2,0:T(8,128)} %copy.42) | copy-start | bytes 3932164
  174.5 8.0 %slice-start.1 = ((s8[6553600]{0:T(1024)(128)(4,1)}), s8[4194304]{0:T(1024)(128)(4,1)S(1)}, s32[]{:S(2)}) async-start(s8[6553600]{0:T(1024)(128)(4,1)} %bitcast.103), calls=%async_computation.1 | async-start | bytes 8388608
  182.3 4.3 slice-start.2
  182.5 4.1 slice-start.3
  186.7 1.3 copy-start.6
  188.0 3.8 copy-start.2
  195.2 61.4 %collective-permute-start.5 = (bf16[2,1,20,128,128]{3,4,2,1,0:T(8,128)(2,1)}, bf16[2,1,20,128,128]{3,4,2,1,0:T(8,128)(2,1)S(1)}, u32[]{:S(2)}, u32[]{:S(2)}) collective-permute-start(bf16[2,1,20,128,128]{3,4,2,1,0:T(8,128)(2,1)} %pad_maximum_fusion.2), channel_id=1, source_target_pairs={{0,4},{4,8},{8,12},{12,16},{16,20},{20,24},{24,28},{28,32},{32,36}... | collective-permute-start | bytes 3932168 | tf_op jit(solution)/shard_map/ppermute | solution.py:20
  229.3 114.3 %collective-permute-start.6 = (bf16[2,1,20,128,128]{3,4,2,1,0:T(8,128)(2,1)}, bf16[2,1,20,128,128]{3,4,2,1,0:T(8,128)(2,1)}, u32[]{:S(2)}, u32[]{:S(2)}) collective-permute-start(bf16[2,1,20,128,128]{3,4,2,1,0:T(8,128)(2,1)} %pad_maximum_fusion.3), channel_id=1, source_target_pairs={{8,0},{12,4},{16,8},{20,12},{24,16},{28,20},{32,24},{36,28},{40,32... | collective-permute-start | bytes 3932168 | tf_op jit(solution)/shard_map/ppermute | solution.py:20
  231.8 111.9 %collective-permute-start.7 = (bf16[2,1,20,128,128]{3,4,2,1,0:T(8,128)(2,1)}, bf16[2,1,20,128,128]{3,4,2,1,0:T(8,128)(2,1)}, u32[]{:S(2)}, u32[]{:S(2)}) collective-permute-start(bf16[2,1,20,128,128]{3,4,2,1,0:T(8,128)(2,1)} %pad_maximum_fusion.4), channel_id=1, source_target_pairs={{0,8},{4,12},{8,16},{12,20},{16,24},{20,28},{24,32},{28,36},{32,40... | collective-permute-start | bytes 3932168 | tf_op jit(solution)/shard_map/ppermute | solution.py:20
  244.7 131.6 %collective-permute-start.4 = (bf16[2,1,20,128,128]{3,4,2,1,0:T(8,128)(2,1)}, bf16[2,1,20,128,128]{3,4,2,1,0:T(8,128)(2,1)}, u32[]{:S(2)}, u32[]{:S(2)}) collective-permute-start(bf16[2,1,20,128,128]{3,4,2,1,0:T(8,128)(2,1)} %pad_maximum_fusion.1), channel_id=1, source_target_pairs={{4,0},{8,4},{12,8},{16,12},{20,16},{24,20},{28,24},{32,28},{36,32}... | collective-permute-start | bytes 3932168 | tf_op jit(solution)/shard_map/ppermute | solution.py:20
  379.5 1.3 copy-start.11
where the time goes:
time: 526 us; the launch traced here: 525 us
  waiting for transfers between devices  249 us (47%)
  blocking collectives  141 us (27%)
  starting transfers between devices  64.4 us (12%)
  local copies, waits for them, and re-layouts  28.3 us (5%)
  matrix products  23.2 us (4%)
  other arithmetic  18 us (3%)
    ppermute x8, waiting for transfers between devices, shifted(): return lax.ppermute(block, axis, route)  249 us
    psum x1, blocking collectives, body(): q_sum, k_sum = lax.psum((q_term, k_term), ('seq', 'dp'))  141 us
    ppermute x8, starting transfers between devices, shifted(): return lax.ppermute(block, axis, route)  64.4 us
    unnamed x45, local copies, waits for them, and re-layouts  21.1 us
  transfers between devices with their start and end apart: 8, of which 6 were waited for; matrix products, arithmetic and copies ran while one was open for 3% of the time, Pallas kernels for 0%

commit v1 on v0

v1 whole, which is shorter than its diff:
```python
import functools
import math

import jax
import jax.numpy as jnp
from jax import lax
from jax.experimental import pallas as pl
from jax.experimental.pallas import tpu as pltpu
from jax.sharding import PartitionSpec as P

HEADS = 20
HEAD_DIM = 128
BLOCK = 128
WIDTH = HEADS * HEAD_DIM
RING = 4
HOME = HEADS // RING
WINDOW = 5
CHAIN = RING + 4
ROWS = 16
SLOT_OF = (3, 1, 0, 2, 4)
EPSILON = 1e-06
SCALE = 1.0 / math.sqrt(HEAD_DIM)
MASKED = -1e30
MESH = pl.DeviceIdType.MESH


def kernel(
    sizes,
    q_ref, k_ref, v_ref, g_ref, q_gain_ref, k_gain_ref, kv_ref,
    dq_out, dk_out, dv_out, gain_out,
    raw, sent, inv, bias, kv, qg, acc, halo_out, halo_in, back, ret, fin,
    gain_own, gain_dp, gain_x, gain_z,
    load_sem, own_sem, fwd_send, fwd_recv, bias_send, bias_recv,
    halo_send, halo_recv, hg_send, hg_recv, ret_send, ret_recv, ret_own,
    gain_send, gain_recv, store_sem,
):
    n_x, n_z, n_dp = sizes
    n_seq = n_x * n_z * RING
    seq = lax.axis_index("seq")
    dp = lax.axis_index("dp")
    me = lax.rem(seq, RING)
    row = seq // RING
    x = lax.rem(row, n_x)
    z = row // n_x

    def ring(t):
        return (row * RING + t, dp)

    def side(s):
        step = n_seq - RING if s == 0 else RING
        return (lax.rem(seq + step, n_seq), dp)

    def at_x(t):
        return ((z * n_x + t) * RING + me, dp)

    def at_z(t):
        return ((t * n_x + x) * RING + me, dp)

    def ahead(d):
        return lax.rem(me + d, RING)

    def behind(d):
        return lax.rem(me + RING - d, RING)

    def head_cols(home, h):
        return pl.ds(pl.multiple_of((home * HOME + h) * HEAD_DIM, HEAD_DIM), HEAD_DIM)

    def chain_rows(block, count=1):
        return pl.ds(pl.multiple_of((block + 2) * BLOCK, BLOCK), count * BLOCK)

    loads = [
        pltpu.make_async_copy(k_ref, raw.at[0], load_sem.at[0]),
        pltpu.make_async_copy(q_ref, raw.at[1], load_sem.at[1]),
        pltpu.make_async_copy(v_ref, sent.at[1], load_sem.at[2]),
        pltpu.make_async_copy(g_ref, sent.at[3], load_sem.at[3]),
    ]
    for load in loads:
        load.start()

    partners = [ring(ahead(d)) for d in range(1, RING)] + [side(0), side(1)]
    partners += [(seq, lax.rem(dp + d, n_dp)) for d in range(1, n_dp)]
    partners += [at_x(lax.rem(x + d, n_x)) for d in range(1, n_x)]
    partners += [at_z(lax.rem(z + d, n_z)) for d in range(1, n_z)]
    barrier = pltpu.get_barrier_semaphore()
    for partner in partners:
        pl.semaphore_signal(barrier, 1, device_id=partner, device_id_type=MESH)

    def normed(which, gain_ref):
        def step(i, carry):
            rows = pl.ds(pl.multiple_of(i * ROWS, ROWS), ROWS)
            value = raw[which, rows, :].astype(jnp.float32)
            mean = jnp.sum(value * value, axis=-1, keepdims=True) * (1.0 / WIDTH)
            scale = lax.rsqrt(mean + EPSILON)
            inv[which, rows, :] = jnp.broadcast_to(scale, (ROWS, HEAD_DIM))
            sent[2 * which, rows, :] = (value * scale * gain_ref[...]).astype(jnp.bfloat16)
            return carry

        lax.fori_loop(0, BLOCK // ROWS, step, 0)

    bias[me] = jnp.zeros((8, HEAD_DIM), jnp.float32)
    for w in range(WINDOW):
        level = jnp.where(kv_ref[0, SLOT_OF[w]] >= 0, 0.0, MASKED).astype(jnp.float32)
        bias[me, w : w + 1, :] = jnp.full((1, HEAD_DIM), level, jnp.float32)

    def bias_copy(d):
        return pltpu.make_async_remote_copy(
            bias.at[me], bias.at[me], bias_send.at[d - 1], bias_recv.at[d - 1],
            device_id=ring(ahead(d)), device_id_type=MESH,
        )

    def bias_arrival(d):
        return pltpu.make_async_remote_copy(
            bias.at[behind(d)], bias.at[behind(d)], bias_send.at[d - 1], bias_recv.at[d - 1],
            device_id=ring(ahead(d)), device_id_type=MESH,
        )

    def forward(h, d, g):
        home = ahead(d)
        source = sent.at[pl.ds(2 * g, 2), :, head_cols(home, h)]
        target = kv.at[h, :, chain_rows(me), :] if g == 0 else qg.at[h, me]
        return pltpu.make_async_remote_copy(
            source, target, fwd_send.at[h, d - 1, g], fwd_recv.at[h, d - 1, g],
            device_id=ring(home), device_id_type=MESH,
        )

    def arrival(h, d, g):
        home = behind(d)
        target = kv.at[h, :, chain_rows(home), :] if g == 0 else qg.at[h, home]
        return pltpu.make_async_remote_copy(
            target, target, fwd_send.at[h, d - 1, g], fwd_recv.at[h, d - 1, g],
            device_id=ring(ahead(d)), device_id_type=MESH,
        )

    def own(h, g):
        source = sent.at[pl.ds(2 * g, 2), :, head_cols(me, h)]
        target = kv.at[h, :, chain_rows(me), :] if g == 0 else qg.at[h, me]
        return pltpu.make_async_copy(source, target, own_sem.at[h, g])

    def halo(h, s):
        mine = pl.ds((2 if s == 0 else RING) * BLOCK, 2 * BLOCK)
        theirs = pl.ds((RING + 2 if s == 0 else 0) * BLOCK, 2 * BLOCK)
        return pltpu.make_async_remote_copy(
            kv.at[h, :, mine, :], kv.at[h, :, theirs, :], halo_send.at[h, s], halo_recv.at[h, s],
            device_id=side(s), device_id_type=MESH,
        )

    def halo_back(h, s):
        return pltpu.make_async_remote_copy(
            halo_out.at[h, s], halo_in.at[h, 1 - s], hg_send.at[h, s], hg_recv.at[h, s],
            device_id=side(s), device_id_type=MESH,
        )

    def give_back(h, d):
        home = ahead(d)
        return pltpu.make_async_remote_copy(
            back.at[h, home], ret.at[:, :, head_cols(me, h)], ret_send.at[h, d - 1], ret_recv.at[h, d - 1],
            device_id=ring(home), device_id_type=MESH,
        )

    def given(h, d):
        target = ret.at[:, :, head_cols(behind(d), h)]
        return pltpu.make_async_remote_copy(
            target, target, ret_send.at[h, d - 1], ret_recv.at[h, d - 1],
            device_id=ring(ahead(d)), device_id_type=MESH,
        )

    def keep_back(h):
        return pltpu.make_async_copy(back.at[h, me], ret.at[:, :, head_cols(me, h)], ret_own.at[h])

    loads[0].wait()
    normed(0, k_gain_ref)
    loads[1].wait()
    normed(1, q_gain_ref)
    loads[2].wait()
    loads[3].wait()
    pl.semaphore_wait(barrier, len(partners))

    for d in range(1, RING):
        bias_copy(d).start()

    def send_head(h, carry):
        for g in range(2):
            for d in (2, 1, 3):
                forward(h, d, g).start()
            own(h, g).start()
        return carry

    lax.fori_loop(0, HOME, send_head, 0)
    for d in range(1, RING):
        bias_arrival(d).wait_recv()

    factor = SCALE * math.log2(math.e)
    by_row = (((1,), (1,)), ((), ()))
    by_col = (((0,), (0,)), ((), ()))

    def return_head(h):
        for d in (2, 1, 3):
            give_back(h, d).start()
        keep_back(h).start()

    def work(h, hold):
        for g in range(2):
            own(h, g).wait()
            for d in range(1, RING):
                arrival(h, d, g).wait_recv()
            if g == 0:
                for s in range(2):
                    halo(h, s).start()
        hold()
        acc[...] = jnp.zeros_like(acc)
        for s in range(2):
            halo(h, s).wait_recv()
        gain_q = jnp.zeros((1, HEAD_DIM), jnp.float32)
        for b in range(RING):
            span = slice(b * BLOCK, (b + WINDOW) * BLOCK)
            keys = kv[h, 0, span, :]
            vals = kv[h, 1, span, :]
            query = qg[h, b, 0]
            grad = qg[h, b, 1]
            level = bias[b][:WINDOW].reshape(WINDOW, 1, HEAD_DIM)
            score = lax.dot_general(keys, query, by_row, preferred_element_type=jnp.float32)
            score = score.reshape(WINDOW, BLOCK, HEAD_DIM) * factor + level
            score = score.reshape(WINDOW * BLOCK, HEAD_DIM)
            top = jnp.max(score, axis=0, keepdims=True)
            weight = jnp.exp2(score - top)
            prob = weight * (1.0 / jnp.sum(weight, axis=0, keepdims=True))
            d_prob = lax.dot_general(vals, grad, by_row, preferred_element_type=jnp.float32)
            delta = jnp.sum(prob * d_prob, axis=0, keepdims=True)
            d_score = (prob * (d_prob - delta)).astype(jnp.bfloat16)
            acc[0, span, :] += jnp.dot(d_score, query, preferred_element_type=jnp.float32)
            acc[1, span, :] += jnp.dot(
                prob.astype(jnp.bfloat16), grad, preferred_element_type=jnp.float32
            )
            d_query = lax.dot_general(d_score, keys, by_col, preferred_element_type=jnp.float32) * SCALE
            back[h, b, 0] = d_query.astype(jnp.bfloat16)
            gain_q += jnp.sum(d_query * query.astype(jnp.float32), axis=0, keepdims=True)
        gain_k = jnp.zeros((1, HEAD_DIM), jnp.float32)
        for c in range(CHAIN):
            part = slice(c * BLOCK, (c + 1) * BLOCK)
            gain_k += jnp.sum(acc[0, part, :] * kv[h, 0, part, :].astype(jnp.float32), axis=0, keepdims=True)
        for s in range(2):
            part = slice(0, 2 * BLOCK) if s == 0 else slice((RING + 2) * BLOCK, CHAIN * BLOCK)
            halo_out[h, s, 0] = (acc[0, part, :] * SCALE).astype(jnp.bfloat16)
            halo_out[h, s, 1] = acc[1, part, :].astype(jnp.bfloat16)
            halo_back(h, s).start()
        gain_own[pl.ds(h, 1), :] = gain_q / q_gain_ref[:, head_cols(me, h)]
        gain_own[pl.ds(h + 8, 1), :] = gain_k * SCALE / k_gain_ref[:, head_cols(me, h)]

    def settle(h):
        for s in range(2):
            halo_back(h, s).wait_recv()
        for b in range(RING):
            part = slice((b + 2) * BLOCK, (b + 3) * BLOCK)
            came = slice((b % 2) * BLOCK, (b % 2 + 1) * BLOCK)
            for t in range(2):
                extra = halo_in[h, b // 2, t, came, :].astype(jnp.float32)
                own_part = acc[t, part, :]
                if t == 0:
                    own_part = own_part * SCALE
                back[h, b, t + 1] = (own_part + extra).astype(jnp.bfloat16)

    gain_own[...] = jnp.zeros_like(gain_own)

    def early(h, carry):
        work(h, lambda: None)
        settle(h)
        return carry

    lax.fori_loop(0, HOME - 1, early, 0)

    def release():
        def step(h, carry):
            return_head(h)
            return carry

        lax.fori_loop(0, HOME - 1, step, 0)

    last = HOME - 1
    work(last, release)

    gain_stages = (
        (gain_dp, dp, n_dp, lambda t: (seq, t), 0),
        (gain_x, x, n_x, at_x, n_dp),
        (gain_z, z, n_z, at_z, n_dp + n_x),
        (fin, me, RING, ring, n_dp + n_x + n_z),
    )

    def gain_copy(stage, d, mine):
        slots, place, count, device, base = gain_stages[stage]
        slot = slots.at[place if mine else lax.rem(place + count - d, count)]
        return pltpu.make_async_remote_copy(
            slot, slot, gain_send.at[base + d], gain_recv.at[base + d],
            device_id=device(lax.rem(place + d, count)), device_id_type=MESH,
        )

    def gain_start(stage, value):
        slots, place, count = gain_stages[stage][:3]
        slots[place] = value
        for d in range(1, count):
            gain_copy(stage, d, True).start()

    def gain_finish(stage):
        slots, count = gain_stages[stage][0], gain_stages[stage][2]
        for d in range(1, count):
            gain_copy(stage, d, False).wait_recv()
        total = slots[0]
        for t in range(1, count):
            total = total + slots[t]
        return total

    gain_start(0, gain_own[...])
    settle(last)
    return_head(last)
    gain_start(1, gain_finish(0))
    gain_start(2, gain_finish(1))
    n_tokens = n_seq * BLOCK * n_dp
    gain_start(3, gain_finish(2) * (1.0 / math.sqrt(n_tokens)))

    def await_head(h, carry):
        for d in range(1, RING):
            given(h, d).wait_recv()
        keep_back(h).wait()
        return carry

    lax.fori_loop(0, HOME, await_head, 0)
    values_out = pltpu.make_async_copy(ret.at[2], dv_out, store_sem)
    values_out.start()

    def finish(which, gain_ref, out_ref):
        def step(i, carry):
            rows = pl.ds(pl.multiple_of(i * ROWS, ROWS), ROWS)
            value = raw[1 - which, rows, :].astype(jnp.float32)
            scaled = gain_ref[...] * ret[which, rows, :].astype(jnp.float32)
            mean = jnp.sum(scaled * value, axis=-1, keepdims=True) * (1.0 / WIDTH)
            scale = inv[1 - which, rows, :][:, :1]
            out_ref[rows, :] = (scale * scaled - value * (scale * scale * scale * mean)).astype(jnp.bfloat16)
            return carry

        lax.fori_loop(0, BLOCK // ROWS, step, 0)

    finish(0, q_gain_ref, dq_out)
    finish(1, k_gain_ref, dk_out)
    gain_finish(3)
    for t in range(RING):
        gain_out[t] = fin[t]
    values_out.wait()

    for d in range(1, RING):
        bias_copy(d).wait_send()

    def drain(h, carry):
        for d in range(1, RING):
            for g in range(2):
                forward(h, d, g).wait_send()
            give_back(h, d).wait_send()
        for s in range(2):
            halo(h, s).wait_send()
            halo_back(h, s).wait_send()
        return carry

    lax.fori_loop(0, HOME, drain, 0)
    for stage in range(4):
        for d in range(1, gain_stages[stage][2]):
            gain_copy(stage, d, True).wait_send()


def body(sizes, q_raw, k_raw, values, d_attn, q_gain, k_gain, kv_lists):
    n_x, n_z, n_dp = sizes
    flat = (BLOCK, WIDTH)
    half = jnp.bfloat16
    anywhere = pl.BlockSpec(memory_space=pl.ANY)
    vmem = pl.BlockSpec(memory_space=pltpu.VMEM)
    dma = pltpu.SemaphoreType.DMA
    n_gain = n_dp + n_x + n_z + RING
    pair = (2, 2 * BLOCK, HEAD_DIM)
    d_q, d_k, d_v, gains = pl.pallas_call(
        functools.partial(kernel, sizes),
        out_shape=(
            jax.ShapeDtypeStruct(flat, half),
            jax.ShapeDtypeStruct(flat, half),
            jax.ShapeDtypeStruct(flat, half),
            jax.ShapeDtypeStruct((RING, 16, HEAD_DIM), jnp.float32),
        ),
        in_specs=[anywhere] * 4 + [vmem, vmem, pl.BlockSpec(memory_space=pltpu.SMEM)],
        out_specs=(vmem, vmem, anywhere, vmem),
        scratch_shapes=[
            pltpu.VMEM((2,) + flat, half),
            pltpu.VMEM((4,) + flat, half),
            pltpu.VMEM((2, BLOCK, HEAD_DIM), jnp.float32),
            pltpu.VMEM((RING, 8, HEAD_DIM), jnp.float32),
            pltpu.VMEM((HOME, 2, CHAIN * BLOCK, HEAD_DIM), half),
            pltpu.VMEM((HOME, RING, 2, BLOCK, HEAD_DIM), half),
            pltpu.VMEM((2, CHAIN * BLOCK, HEAD_DIM), jnp.float32),
            pltpu.VMEM((HOME, 2) + pair, half),
            pltpu.VMEM((HOME, 2) + pair, half),
            pltpu.VMEM((HOME, RING, 3, BLOCK, HEAD_DIM), half),
            pltpu.VMEM((3,) + flat, half),
            pltpu.VMEM((RING, 16, HEAD_DIM), jnp.float32),
            pltpu.VMEM((16, HEAD_DIM), jnp.float32),
            pltpu.VMEM((n_dp, 16, HEAD_DIM), jnp.float32),
            pltpu.VMEM((n_x, 16, HEAD_DIM), jnp.float32),
            pltpu.VMEM((n_z, 16, HEAD_DIM), jnp.float32),
            dma((4,)),
            dma((HOME, 2)),
            dma((HOME, RING - 1, 2)),
            dma((HOME, RING - 1, 2)),
            dma((RING - 1,)),
            dma((RING - 1,)),
            dma((HOME, 2)),
            dma((HOME, 2)),
            dma((HOME, 2)),
            dma((HOME, 2)),
            dma((HOME, RING - 1)),
            dma((HOME, RING - 1)),
            dma((HOME,)),
            dma((n_gain,)),
            dma((n_gain,)),
            dma,
        ],
        compiler_params=pltpu.CompilerParams(
            collective_id=0, has_side_effects=True, vmem_limit_bytes=40 * 1024 * 1024
        ),
    )(
        q_raw.reshape(flat), k_raw.reshape(flat), values.reshape(flat), d_attn.reshape(flat),
        q_gain.reshape(1, WIDTH), k_gain.reshape(1, WIDTH), kv_lists,
    )
    shape = q_raw.shape
    q_sum = gains[:, :HOME].reshape(WIDTH)
    k_sum = gains[:, 8 : 8 + HOME].reshape(WIDTH)
    return d_q.reshape(shape), d_k.reshape(shape), d_v.reshape(shape), q_sum, k_sum


def solution(mesh):
    rows = mesh.shape["seq"] // RING
    n_x = 4 if rows % 4 == 0 and rows > 4 else 2
    sizes = (n_x, rows // n_x, mesh.shape["dp"])
    split = P("dp", "seq", None)
    return jax.shard_map(
        functools.partial(body, sizes),
        mesh=mesh,
        in_specs=(split, split, split, split, P(), P(), P("seq", None)),
        out_specs=(split, split, split, P(), P()),
        check_vma=False,
    )
```

time: 526 us -> 151 us (0.29)
  the two profiles are of different devices: /device:TPU:1 before, /device:TPU:8 now
where the time goes in v1:
time: 151 us
  Pallas kernels  140 us (93%)
  local copies, waits for them, and re-layouts  9.45 us (6%)
    pallas_call x1, Pallas kernels, body(): pl.pallas_call(functools.partial(kernel, sizes), out_shape=(jax.ShapeDtyp...  140 us
    unnamed x15, local copies, waits for them, and re-layouts  7.51 us

profile of v1, /device:TPU:8, one launch (start us, length us, event | category | flops | bytes accessed | tf_op | source)
XLA Modules:
  0.0 150.5 jit_solution(14276148323814603354)
XLA Ops:
  0.6 0.0 copy-start.5
  0.6 0.7 reshape.47.q_gain_ref
  1.4 0.0 copy-done.5
  1.4 0.0 copy-start.4
  1.4 0.6 copy-done.4
  2.0 0.0 copy-start
  2.0 1.1 copy-done
  3.1 0.0 copy-start.1
  3.1 1.1 copy-done.1
  4.2 0.0 copy-start.2
  4.2 1.1 copy-done.2
  5.3 0.0 copy-start.3
  5.3 1.1 copy-done.3
  6.4 140.4 %shard_map.110 = (bf16[128,2560]{1,0:T(8,128)(2,1)S(1)}, bf16[128,2560]{1,0:T(8,128)(2,1)S(1)}, bf16[128,2560]{1,0:T(8,128)(2,1)S(1)}, f32[4,16,128]{2,1,0:T(8,128)S(1)}) custom-call(bf16[128,2560]{1,0:T(8,128)(2,1)S(1)} %bitcast.10, bf16[128,2560]{1,0:T(8,128)(2,1)S(1)} %bitcast.11, bf16[128,2560]{1,0:T(8,128)(2,1)S(1)} %bitcast.12, ...), custom_call_target="tpu_custom_call" | custom-call | tf_op jit(solution)/shard_map/pallas_call | solution.py:376
  146.8 0.6 reshape.52
  147.4 0.6 reshape.53
  148.0 0.8 copy.15
  148.8 0.8 copy.16
  149.7 0.8 copy.17
  (2 shorter events, 0.0 us)
Async XLA Ops:
  0.6 0.7 copy-start.5
  1.4 0.7 copy-start.4
  2.0 1.1 copy-start
  3.1 1.1 copy-start.1
  4.2 1.1 copy-start.2
  5.3 1.1 copy-start.3

commit v2 on v1

v2 whole, which is shorter than its diff:
```python
import functools
import math

import jax
import jax.numpy as jnp
from jax import lax
from jax.experimental import pallas as pl
from jax.experimental.pallas import tpu as pltpu
from jax.sharding import PartitionSpec as P

HEADS = 20
HEAD_DIM = 128
BLOCK = 128
WIDTH = HEADS * HEAD_DIM
RING = 4
HOME = HEADS // RING
WINDOW = 5
CHAIN = RING + 4
ROWS = 16
SLOT_OF = (3, 1, 0, 2, 4)
EPSILON = 1e-06
SCALE = 1.0 / math.sqrt(HEAD_DIM)
MASKED = -1e30
MESH = pl.DeviceIdType.MESH


def kernel(
    sizes,
    q_ref, k_ref, v_ref, g_ref, q_gain_ref, k_gain_ref, kv_ref,
    dq_out, dk_out, dv_out, gain_out,
    raw, sent, inv, gains, bias_own, bias, chain, acc, halo_out, halo_in, back, ret, fin,
    gain_own, gain_dp, gain_x, gain_z,
    load_sem, fwd_send, fwd_recv, bias_send, bias_recv,
    halo_send, halo_recv, hg_send, hg_recv, ret_send, ret_recv,
    gain_send, gain_recv, store_sem,
):
    n_x, n_z, n_dp = sizes
    n_seq = n_x * n_z * RING
    seq = lax.axis_index("seq")
    dp = lax.axis_index("dp")
    me = lax.rem(seq, RING)
    row = seq // RING
    x = lax.rem(row, n_x)
    z = row // n_x

    across = lax.rem(dp + n_dp // 2, n_dp)

    def ring(t):
        return (row * RING + t, dp)

    def over(t):
        return (row * RING + t, across)

    def side(s):
        step = n_seq - RING if s == 0 else RING
        return (lax.rem(seq + step, n_seq), dp)

    def at_x(t):
        return ((z * n_x + t) * RING + me, dp)

    def at_z(t):
        return ((t * n_x + x) * RING + me, dp)

    def ahead(d):
        return lax.rem(me + d, RING)

    def behind(d):
        return lax.rem(me + RING - d, RING)

    def head_cols(home, h):
        return pl.ds(pl.multiple_of((home * HOME + h) * HEAD_DIM, HEAD_DIM), HEAD_DIM)

    def chain_rows(block, count=1):
        return pl.ds(pl.multiple_of((block + 2) * BLOCK, BLOCK), count * BLOCK)

    loads = [
        pltpu.make_async_copy(k_ref, raw.at[0], load_sem.at[0]),
        pltpu.make_async_copy(q_ref, raw.at[1], load_sem.at[1]),
        pltpu.make_async_copy(g_ref, sent.at[0], load_sem.at[2]),
        pltpu.make_async_copy(v_ref, sent.at[1], load_sem.at[3]),
    ]
    for load in loads:
        load.start()

    partners = [over(t) for t in range(RING)] + [side(0), side(1)]
    partners += [ring(ahead(d)) for d in range(1, RING)]
    partners += [(seq, lax.rem(dp + d, n_dp)) for d in range(1, n_dp)]
    partners += [at_x(lax.rem(x + d, n_x)) for d in range(1, n_x)]
    partners += [at_z(lax.rem(z + d, n_z)) for d in range(1, n_z)]
    barrier = pltpu.get_barrier_semaphore()
    for partner in partners:
        pl.semaphore_signal(barrier, 1, device_id=partner, device_id_type=MESH)

    gains[0] = k_gain_ref[...].reshape(1, WIDTH)
    gains[1] = q_gain_ref[...].reshape(1, WIDTH)

    def normed(which):
        def step(i, carry):
            rows = pl.ds(pl.multiple_of(i * ROWS, ROWS), ROWS)
            value = raw[which, rows, :].astype(jnp.float32)
            mean = jnp.sum(value * value, axis=-1, keepdims=True) * (1.0 / WIDTH)
            scale = lax.rsqrt(mean + EPSILON)
            inv[which, rows, :] = jnp.broadcast_to(scale, (ROWS, HEAD_DIM))
            sent[2 + which, rows, :] = (value * scale * gains[which]).astype(jnp.bfloat16)
            return carry

        lax.fori_loop(0, BLOCK // ROWS, step, 0)

    bias_own[...] = jnp.zeros((8, HEAD_DIM), jnp.float32)
    for w in range(WINDOW):
        level = jnp.where(kv_ref[0, SLOT_OF[w]] >= 0, 0.0, MASKED).astype(jnp.float32)
        bias_own[w : w + 1, :] = jnp.full((1, HEAD_DIM), level, jnp.float32)

    def bias_copy(d):
        return pltpu.make_async_remote_copy(
            bias_own, bias.at[me], bias_send.at[d], bias_recv.at[d],
            device_id=over(ahead(d)), device_id_type=MESH,
        )

    def bias_arrival(d):
        return pltpu.make_async_remote_copy(
            bias_own, bias.at[behind(d)], bias_send.at[d], bias_recv.at[d],
            device_id=over(ahead(d)), device_id_type=MESH,
        )

    def forward(h, d, g):
        home = ahead(d)
        part = pl.ds(2 * g, 2)
        return pltpu.make_async_remote_copy(
            sent.at[part, :, head_cols(home, h)], chain.at[h, part, chain_rows(me), :],
            fwd_send.at[h, d, g], fwd_recv.at[h, d, g],
            device_id=over(home), device_id_type=MESH,
        )

    def arrival(h, d, g):
        target = chain.at[h, pl.ds(2 * g, 2), chain_rows(behind(d)), :]
        return pltpu.make_async_remote_copy(
            target, target, fwd_send.at[h, d, g], fwd_recv.at[h, d, g],
            device_id=over(ahead(d)), device_id_type=MESH,
        )

    def halo(h, s):
        mine = pl.ds((2 if s == 0 else RING) * BLOCK, 2 * BLOCK)
        theirs = pl.ds((RING + 2 if s == 0 else 0) * BLOCK, 2 * BLOCK)
        return pltpu.make_async_remote_copy(
            chain.at[h, 1:3, mine, :], chain.at[h, 1:3, theirs, :], halo_send.at[h, s], halo_recv.at[h, s],
            device_id=side(s), device_id_type=MESH,
        )

    def halo_back(h, s):
        return pltpu.make_async_remote_copy(
            halo_out.at[h, s], halo_in.at[h, 1 - s], hg_send.at[h, s], hg_recv.at[h, s],
            device_id=side(s), device_id_type=MESH,
        )

    def target_of(t, home, h):
        cols = head_cols(home, h)
        return ret.at[:, :, cols] if t == 0 else dv_out.at[:, cols]

    def give_back(h, d, t):
        home = ahead(d)
        return pltpu.make_async_remote_copy(
            back.at[h, home, 0:2] if t == 0 else back.at[h, home, 2], target_of(t, me, h),
            ret_send.at[h, d, t], ret_recv.at[h, d, t],
            device_id=over(home), device_id_type=MESH,
        )

    def given(h, d, t):
        target = target_of(t, behind(d), h)
        return pltpu.make_async_remote_copy(
            target, target, ret_send.at[h, d, t], ret_recv.at[h, d, t],
            device_id=over(ahead(d)), device_id_type=MESH,
        )

    loads[0].wait()
    normed(0)
    loads[1].wait()
    normed(1)
    loads[2].wait()
    loads[3].wait()
    pl.semaphore_wait(barrier, len(partners))

    def send_head(h, carry):
        for g in range(2):
            for d in range(RING):
                forward(h, d, g).start()
        return carry

    send_head(0, 0)
    for d in range(RING):
        bias_copy(d).start()
    send_head(1, 0)

    factor = SCALE * math.log2(math.e)
    by_row = (((1,), (1,)), ((), ()))
    by_col = (((0,), (0,)), ((), ()))

    def return_head(h, t):
        for d in range(RING):
            give_back(h, d, t).start()

    def receive(h):
        for g in range(2):
            for d in range(RING):
                arrival(h, d, g).wait_recv()
        for s in range(2):
            halo(h, s).start()

    def work(h):
        acc[...] = jnp.zeros_like(acc)
        for s in range(2):
            halo(h, s).wait_recv()
        gain_q = jnp.zeros((1, HEAD_DIM), jnp.float32)
        for b in range(RING):
            span = slice(b * BLOCK, (b + WINDOW) * BLOCK)
            mine = slice((b + 2) * BLOCK, (b + 3) * BLOCK)
            vals = chain[h, 1, span, :]
            keys = chain[h, 2, span, :]
            grad = chain[h, 0, mine, :]
            query = chain[h, 3, mine, :]
            level = bias[b][:WINDOW].reshape(WINDOW, 1, HEAD_DIM)
            score = lax.dot_general(keys, query, by_row, preferred_element_type=jnp.float32)
            score = score.reshape(WINDOW, BLOCK, HEAD_DIM) * factor + level
            score = score.reshape(WINDOW * BLOCK, HEAD_DIM)
            top = jnp.max(score, axis=0, keepdims=True)
            weight = jnp.exp2(score - top)
            prob = weight * (1.0 / jnp.sum(weight, axis=0, keepdims=True))
            d_prob = lax.dot_general(vals, grad, by_row, preferred_element_type=jnp.float32)
            delta = jnp.sum(prob * d_prob, axis=0, keepdims=True)
            d_score = (prob * (d_prob - delta)).astype(jnp.bfloat16)
            acc[0, span, :] += jnp.dot(d_score, query, preferred_element_type=jnp.float32)
            acc[1, span, :] += jnp.dot(
                prob.astype(jnp.bfloat16), grad, preferred_element_type=jnp.float32
            )
            d_query = lax.dot_general(d_score, keys, by_col, preferred_element_type=jnp.float32) * SCALE
            back[h, b, 0] = d_query.astype(jnp.bfloat16)
            gain_q += jnp.sum(d_query * query.astype(jnp.float32), axis=0, keepdims=True)
        gain_k = jnp.zeros((1, HEAD_DIM), jnp.float32)
        for c in range(CHAIN):
            part = slice(c * BLOCK, (c + 1) * BLOCK)
            gain_k += jnp.sum(acc[0, part, :] * chain[h, 2, part, :].astype(jnp.float32), axis=0, keepdims=True)
        for s in range(2):
            part = slice(0, 2 * BLOCK) if s == 0 else slice((RING + 2) * BLOCK, CHAIN * BLOCK)
            halo_out[h, s, 0] = (acc[0, part, :] * SCALE).astype(jnp.bfloat16)
            halo_out[h, s, 1] = acc[1, part, :].astype(jnp.bfloat16)
            halo_back(h, s).start()
        gain_own[pl.ds(h, 1), :] = gain_q / gains[1, :, head_cols(me, h)]
        gain_own[pl.ds(h + 8, 1), :] = gain_k * SCALE / gains[0, :, head_cols(me, h)]

    def settle(h):
        for s in range(2):
            halo_back(h, s).wait_recv()
        for b in range(RING):
            part = slice((b + 2) * BLOCK, (b + 3) * BLOCK)
            came = slice((b % 2) * BLOCK, (b % 2 + 1) * BLOCK)
            for t in range(2):
                extra = halo_in[h, b // 2, t, came, :].astype(jnp.float32)
                own_part = acc[t, part, :]
                if t == 0:
                    own_part = own_part * SCALE
                back[h, b, t + 1] = (own_part + extra).astype(jnp.bfloat16)

    gain_own[...] = jnp.zeros_like(gain_own)

    last = HOME - 1
    receive(0)
    send_head(2, 0)
    for d in range(RING):
        bias_arrival(d).wait_recv()
    work(0)

    def middle(h, carry):
        receive(h)

        @pl.when(h + 2 < HOME)
        def _():
            send_head(h + 2, 0)

        settle(h - 1)
        return_head(h - 1, 0)
        work(h)
        return carry

    lax.fori_loop(1, last, middle, 0)
    receive(last)
    settle(last - 1)
    return_head(last - 1, 0)
    work(last)

    gain_stages = (
        (gain_dp, dp, n_dp, lambda t: (seq, t), 0),
        (gain_x, x, n_x, at_x, n_dp),
        (gain_z, z, n_z, at_z, n_dp + n_x),
        (fin, me, RING, ring, n_dp + n_x + n_z),
    )

    def gain_copy(stage, d, mine):
        slots, place, count, device, base = gain_stages[stage]
        slot = slots.at[place if mine else lax.rem(place + count - d, count)]
        return pltpu.make_async_remote_copy(
            slot, slot, gain_send.at[base + d], gain_recv.at[base + d],
            device_id=device(lax.rem(place + d, count)), device_id_type=MESH,
        )

    def gain_start(stage, value):
        slots, place, count = gain_stages[stage][:3]
        slots[place] = value
        for d in range(1, count):
            gain_copy(stage, d, True).start()

    def gain_finish(stage):
        slots, count = gain_stages[stage][0], gain_stages[stage][2]
        for d in range(1, count):
            gain_copy(stage, d, False).wait_recv()
        total = slots[0]
        for t in range(1, count):
            total = total + slots[t]
        return total

    gain_start(0, gain_own[...])
    settle(last)
    return_head(last, 0)
    for h in range(HOME):
        return_head(h, 1)
    gain_start(1, gain_finish(0))
    gain_start(2, gain_finish(1))
    n_tokens = n_seq * BLOCK * n_dp
    gain_start(3, gain_finish(2) * (1.0 / math.sqrt(n_tokens)))

    def await_returns(t):
        def step(h, carry):
            for d in range(RING):
                given(h, d, t).wait_recv()
            return carry

        lax.fori_loop(0, HOME, step, 0)

    await_returns(0)

    def finish(which, out_ref):
        def step(i, carry):
            rows = pl.ds(pl.multiple_of(i * ROWS, ROWS), ROWS)
            value = raw[1 - which, rows, :].astype(jnp.float32)
            scaled = gains[1 - which] * ret[which, rows, :].astype(jnp.float32)
            mean = jnp.sum(scaled * value, axis=-1, keepdims=True) * (1.0 / WIDTH)
            scale = inv[1 - which, rows, :][:, :1]
            ret[which, rows, :] = (scale * scaled - value * (scale * scale * scale * mean)).astype(jnp.bfloat16)
            return carry

        lax.fori_loop(0, BLOCK // ROWS, step, 0)
        store = pltpu.make_async_copy(ret.at[which], out_ref, store_sem.at[which])
        store.start()
        return store

    stores = [finish(0, dq_out), finish(1, dk_out)]
    gain_finish(3)
    for t in range(RING):
        gain_out[t] = fin[t]
    await_returns(1)
    for store in stores:
        store.wait()

    for d in range(RING):
        bias_copy(d).wait_send()

    def drain(h, carry):
        for d in range(RING):
            for g in range(2):
                forward(h, d, g).wait_send()
                give_back(h, d, g).wait_send()
        for s in range(2):
            halo(h, s).wait_send()
            halo_back(h, s).wait_send()
        return carry

    lax.fori_loop(0, HOME, drain, 0)
    for stage in range(4):
        for d in range(1, gain_stages[stage][2]):
            gain_copy(stage, d, True).wait_send()


def hand_over(dq_ref, dk_ref, dv_ref, gain_ref, dq_out, dk_out, dv_out, q_sum, k_sum, held, in_sem, out_sem):
    loads = [
        pltpu.make_async_copy(src, held.at[i], in_sem.at[i]) for i, src in enumerate((dq_ref, dk_ref, dv_ref))
    ]
    stores = [
        pltpu.make_async_copy(held.at[i], dst, out_sem.at[i]) for i, dst in enumerate((dq_out, dk_out, dv_out))
    ]
    for load in loads:
        load.start()
    for load, store in zip(loads, stores):
        load.wait()
        store.start()
    for home in range(RING):
        for h in range(HOME):
            cols = pl.ds((home * HOME + h) * HEAD_DIM, HEAD_DIM)
            q_sum[cols] = gain_ref[home, h]
            k_sum[cols] = gain_ref[home, 8 + h]
    for store in stores:
        store.wait()


def body(sizes, q_raw, k_raw, values, d_attn, q_gain, k_gain, kv_lists):
    n_x, n_z, n_dp = sizes
    flat = (BLOCK, WIDTH)
    half = jnp.bfloat16
    anywhere = pl.BlockSpec(memory_space=pl.ANY)
    vmem = pl.BlockSpec(memory_space=pltpu.VMEM)
    dma = pltpu.SemaphoreType.DMA
    n_gain = n_dp + n_x + n_z + RING
    pair = (2, 2 * BLOCK, HEAD_DIM)
    d_q, d_k, d_v, gains = pl.pallas_call(
        functools.partial(kernel, sizes),
        out_shape=(
            jax.ShapeDtypeStruct(flat, half),
            jax.ShapeDtypeStruct(flat, half),
            jax.ShapeDtypeStruct(flat, half),
            jax.ShapeDtypeStruct((RING, 16, HEAD_DIM), jnp.float32),
        ),
        in_specs=[anywhere] * 4 + [vmem, vmem, pl.BlockSpec(memory_space=pltpu.SMEM)],
        out_specs=(anywhere, anywhere, anywhere, vmem),
        scratch_shapes=[
            pltpu.VMEM((2,) + flat, half),
            pltpu.VMEM((4,) + flat, half),
            pltpu.VMEM((2, BLOCK, HEAD_DIM), jnp.float32),
            pltpu.VMEM((2, 1, WIDTH), jnp.float32),
            pltpu.VMEM((8, HEAD_DIM), jnp.float32),
            pltpu.VMEM((RING, 8, HEAD_DIM), jnp.float32),
            pltpu.VMEM((HOME, 4, CHAIN * BLOCK, HEAD_DIM), half),
            pltpu.VMEM((2, CHAIN * BLOCK, HEAD_DIM), jnp.float32),
            pltpu.VMEM((HOME, 2) + pair, half),
            pltpu.VMEM((HOME, 2) + pair, half),
            pltpu.VMEM((HOME, RING, 3, BLOCK, HEAD_DIM), half),
            pltpu.VMEM((2,) + flat, half),
            pltpu.VMEM((RING, 16, HEAD_DIM), jnp.float32),
            pltpu.VMEM((16, HEAD_DIM), jnp.float32),
            pltpu.VMEM((n_dp, 16, HEAD_DIM), jnp.float32),
            pltpu.VMEM((n_x, 16, HEAD_DIM), jnp.float32),
            pltpu.VMEM((n_z, 16, HEAD_DIM), jnp.float32),
            dma((4,)),
            dma((HOME, RING, 2)),
            dma((HOME, RING, 2)),
            dma((RING,)),
            dma((RING,)),
            dma((HOME, 2)),
            dma((HOME, 2)),
            dma((HOME, 2)),
            dma((HOME, 2)),
            dma((HOME, RING, 2)),
            dma((HOME, RING, 2)),
            dma((n_gain,)),
            dma((n_gain,)),
            dma((2,)),
        ],
        compiler_params=pltpu.CompilerParams(
            collective_id=0, has_side_effects=True, vmem_limit_bytes=62 * 1024 * 1024
        ),
    )(
        q_raw.reshape(flat), k_raw.reshape(flat), values.reshape(flat), d_attn.reshape(flat),
        q_gain, k_gain, kv_lists,
    )
    out = pl.pallas_call(
        hand_over,
        out_shape=(jax.ShapeDtypeStruct(flat, half),) * 3 + (jax.ShapeDtypeStruct((WIDTH,), jnp.float32),) * 2,
        in_specs=[anywhere] * 3 + [vmem],
        out_specs=(anywhere,) * 3 + (vmem,) * 2,
        scratch_shapes=[pltpu.VMEM((3,) + flat, half), dma((3,)), dma((3,))],
    )(d_q, d_k, d_v, gains)
    shape = q_raw.shape
    return tuple(part.reshape(shape) for part in out[:3]) + out[3:]


def solution(mesh):
    rows = mesh.shape["seq"] // RING
    n_x = 4 if rows % 4 == 0 and rows > 4 else 2
    sizes = (n_x, rows // n_x, mesh.shape["dp"])
    split = P("dp", "seq", None)
    return jax.shard_map(
        functools.partial(body, sizes),
        mesh=mesh,
        in_specs=(split, split, split, split, P(), P(), P("seq", None)),
        out_specs=(split, split, split, P(), P()),
        check_vma=False,
    )
```

time: 151 us -> 126 us (0.83)
  the two profiles are of different devices: /device:TPU:8 before, /device:TPU:1 now
where the time goes in v2:
time: 126 us; the launch traced here: 125 us
  Pallas kernels  125 us (99%)
    pallas_call x1, Pallas kernels, body(): pl.pallas_call(functools.partial(kernel, sizes), out_shape=(jax.ShapeDtyp...  121 us
    pallas_call x1, Pallas kernels, body(): pl.pallas_call(hand_over, out_shape=(jax.ShapeDtypeStruct(flat, half),) *...  3.77 us

profile of v2, /device:TPU:1, one launch (start us, length us, event | category | flops | bytes accessed | tf_op | source)
XLA Modules:
  0.0 125.3 jit_solution(16644497158071542001)
XLA Ops:
  0.6 120.9 %shard_map.110 = (bf16[128,2560]{1,0:T(8,128)(2,1)}, bf16[128,2560]{1,0:T(8,128)(2,1)}, bf16[128,2560]{1,0:T(8,128)(2,1)}, f32[4,16,128]{2,1,0:T(8,128)}) custom-call(bf16[128,2560]{1,0:T(8,128)(2,1)} %bitcast.7, bf16[128,2560]{1,0:T(8,128)(2,1)} %bitcast.8, bf16[128,2560]{1,0:T(8,128)(2,1)} %bitcast.9, bf16[128,2560]{1,0:T(8,128)(2,1)} %bitcast.10, ...), custom_call_target="tpu_custom_call" | custom-call | tf_op jit(solution)/shard_map/pallas_call | solution.py:412
  121.5 3.8 %shard_map.111 = (bf16[128,2560]{1,0:T(8,128)(2,1)}, bf16[128,2560]{1,0:T(8,128)(2,1)}, bf16[128,2560]{1,0:T(8,128)(2,1)}, f32[2560]{0:T(1024)}, f32[2560]{0:T(1024)}) custom-call(bf16[128,2560]{1,0:T(8,128)(2,1)} %get-tuple-element.14.dq_ref, bf16[128,2560]{1,0:T(8,128)(2,1)} %get-tuple-element.15.dk_ref, bf16[128,2560]{1,0:T(8,128)(2,1)} %get-tuple-element.16.dv_ref, ...), custom_call_target="tpu_custom_call" | custom-call | tf_op jit(solution)/shard_map/pallas_call | solution.py:462

commit v3 on v2

--- a/solution.py
+++ b/solution.py
@@ -21,6 +21,7 @@
 EPSILON = 1e-06
 SCALE = 1.0 / math.sqrt(HEAD_DIM)
 MASKED = -1e30
+TOKENS = 6
 MESH = pl.DeviceIdType.MESH
 
 
@@ -28,11 +29,11 @@
     sizes,
     q_ref, k_ref, v_ref, g_ref, q_gain_ref, k_gain_ref, kv_ref,
     dq_out, dk_out, dv_out, gain_out,
-    raw, sent, inv, gains, bias_own, bias, chain, acc, halo_out, halo_in, back, ret, fin,
-    gain_own, gain_dp, gain_x, gain_z,
+    raw, sent, inv, k_gain, q_gain, gains, bias_own, bias, chain, acc, halo_out, halo_in, back, ret, fin,
+    gain_own, gain_plane, gain_z,
     load_sem, fwd_send, fwd_recv, bias_send, bias_recv,
     halo_send, halo_recv, hg_send, hg_recv, ret_send, ret_recv,
-    gain_send, gain_recv, store_sem,
+    gain_send, gain_recv, token, store_sem,
 ):
     n_x, n_z, n_dp = sizes
     n_seq = n_x * n_z * RING
@@ -55,8 +56,8 @@
         step = n_seq - RING if s == 0 else RING
         return (lax.rem(seq + step, n_seq), dp)
 
-    def at_x(t):
-        return ((z * n_x + t) * RING + me, dp)
+    def at_plane(t):
+        return ((z * n_x + lax.rem(t, n_x)) * RING + me, t // n_x)
 
     def at_z(t):
         return ((t * n_x + x) * RING + me, dp)
@@ -78,21 +79,44 @@
         pltpu.make_async_copy(q_ref, raw.at[1], load_sem.at[1]),
         pltpu.make_async_copy(g_ref, sent.at[0], load_sem.at[2]),
         pltpu.make_async_copy(v_ref, sent.at[1], load_sem.at[3]),
+        pltpu.make_async_copy(k_gain_ref, k_gain, load_sem.at[4]),
+        pltpu.make_async_copy(q_gain_ref, q_gain, load_sem.at[5]),
     ]
     for load in loads:
         load.start()
 
-    partners = [over(t) for t in range(RING)] + [side(0), side(1)]
+    partners = [over(t) for t in range(RING)]
     partners += [ring(ahead(d)) for d in range(1, RING)]
-    partners += [(seq, lax.rem(dp + d, n_dp)) for d in range(1, n_dp)]
-    partners += [at_x(lax.rem(x + d, n_x)) for d in range(1, n_x)]
-    partners += [at_z(lax.rem(z + d, n_z)) for d in range(1, n_z)]
+    plane = dp * n_x + x
+    partners += [at_plane(lax.rem(plane + d, n_dp * n_x)) for d in range(1, n_dp * n_x)]
+    has_side = (row > 0, row < n_x * n_z - 1)
+    edges = [(has_side[0], side(0)), (has_side[1], side(1))]
+    edges += [(z > 0, at_z(z - 1)), (z < n_z - 1, at_z(z + 1))]
     barrier = pltpu.get_barrier_semaphore()
     for partner in partners:
         pl.semaphore_signal(barrier, 1, device_id=partner, device_id_type=MESH)
-
-    gains[0] = k_gain_ref[...].reshape(1, WIDTH)
-    gains[1] = q_gain_ref[...].reshape(1, WIDTH)
+    for there, partner in edges:
+
+        @pl.when(there)
+        def _(partner=partner):
+            pl.semaphore_signal(barrier, 1, device_id=partner, device_id_type=MESH)
+
+    @pl.when(row == 0)
+    def _():
+        for h in range(HOME):
+            chain[h, 1:3, : 2 * BLOCK, :] = jnp.zeros((2, 2 * BLOCK, HEAD_DIM), jnp.bfloat16)
+            halo_in[h, 0] = jnp.zeros((2, 2 * BLOCK, HEAD_DIM), jnp.bfloat16)
+
+    @pl.when(row == n_x * n_z - 1)
+    def _():
+        for h in range(HOME):
+            chain[h, 1:3, (RING + 2) * BLOCK :, :] = jnp.zeros((2, 2 * BLOCK, HEAD_DIM), jnp.bfloat16)
+            halo_in[h, 1] = jnp.zeros((2, 2 * BLOCK, HEAD_DIM), jnp.bfloat16)
+
+    loads[4].wait()
+    loads[5].wait()
+    gains[0] = k_gain[...].reshape(1, WIDTH)
+    gains[1] = q_gain[...].reshape(1, WIDTH)
 
     def normed(which):
         def step(i, carry):
@@ -178,7 +202,36 @@
     normed(1)
     loads[2].wait()
     loads[3].wait()
-    pl.semaphore_wait(barrier, len(partners))
+    n_rows = n_x * n_z
+    n_edges = (row + n_rows - 1) // n_rows + (2 * n_rows - 2 - row) // n_rows
+    n_edges = n_edges + (z + n_z - 1) // n_z + (2 * n_z - 2 - z) // n_z
+    pl.semaphore_wait(barrier, len(partners) + n_edges)
+
+    def tell(r):
+        for way in range(2):
+
+            @pl.when((z < n_z - 1) if way else (z > 0))
+            def _(way=way):
+                pl.semaphore_signal(
+                    token.at[way, r], 1, device_id=at_z(z + (1 if way else -1)), device_id_type=MESH
+                )
+
+    def hear(r):
+        for way in range(2):
+
+            @pl.when((z > 0) if way else (z < n_z - 1))
+            def _(way=way):
+                pl.semaphore_wait(token.at[way, r], 1)
+
+    def sent_by(s, copy, act):
+        @pl.when(has_side[s])
+        def _():
+            getattr(copy, act)()
+
+    def got_from(s, copy):
+        @pl.when(has_side[1 - s])
+        def _():
+            copy.wait_recv()
 
     def send_head(h, carry):
         for g in range(2):
@@ -186,6 +239,7 @@
                 forward(h, d, g).start()
         return carry
 
+    tell(0)
     send_head(0, 0)
     for d in range(RING):
         bias_copy(d).start()
@@ -204,12 +258,12 @@
             for d in range(RING):
                 arrival(h, d, g).wait_recv()
         for s in range(2):
-            halo(h, s).start()
+            sent_by(s, halo(h, s), "start")
 
     def work(h):
         acc[...] = jnp.zeros_like(acc)
         for s in range(2):
-            halo(h, s).wait_recv()
+            got_from(s, halo(h, s))
         gain_q = jnp.zeros((1, HEAD_DIM), jnp.float32)
         for b in range(RING):
             span = slice(b * BLOCK, (b + WINDOW) * BLOCK)
@@ -243,13 +297,13 @@
             part = slice(0, 2 * BLOCK) if s == 0 else slice((RING + 2) * BLOCK, CHAIN * BLOCK)
             halo_out[h, s, 0] = (acc[0, part, :] * SCALE).astype(jnp.bfloat16)
             halo_out[h, s, 1] = acc[1, part, :].astype(jnp.bfloat16)
-            halo_back(h, s).start()
+            sent_by(s, halo_back(h, s), "start")
         gain_own[pl.ds(h, 1), :] = gain_q / gains[1, :, head_cols(me, h)]
         gain_own[pl.ds(h + 8, 1), :] = gain_k * SCALE / gains[0, :, head_cols(me, h)]
 
     def settle(h):
         for s in range(2):
-            halo_back(h, s).wait_recv()
+            got_from(s, halo_back(h, s))
         for b in range(RING):
             part = slice((b + 2) * BLOCK, (b + 3) * BLOCK)
             came = slice((b % 2) * BLOCK, (b % 2 + 1) * BLOCK)
@@ -271,6 +325,8 @@
 
     def middle(h, carry):
         receive(h)
+        hear(2 * h - 2)
+        tell(2 * h - 1)
 
         @pl.when(h + 2 < HOME)
         def _():
@@ -279,6 +335,12 @@
         settle(h - 1)
         return_head(h - 1, 0)
         work(h)
+        hear(2 * h - 1)
+
+        @pl.when(2 * h < TOKENS)
+        def _():
+            tell(2 * h)
+
         return carry
 
     lax.fori_loop(1, last, middle, 0)
@@ -288,10 +350,9 @@
     work(last)
 
     gain_stages = (
-        (gain_dp, dp, n_dp, lambda t: (seq, t), 0),
-        (gain_x, x, n_x, at_x, n_dp),
-        (gain_z, z, n_z, at_z, n_dp + n_x),
-        (fin, me, RING, ring, n_dp + n_x + n_z),
+        (gain_plane, plane, n_dp * n_x, at_plane, 0),
+        (gain_z, z, n_z, at_z, n_dp * n_x),
+        (fin, me, RING, ring, n_dp * n_x + n_z),
     )
 
     def gain_copy(stage, d, mine):
@@ -322,10 +383,9 @@
     return_head(last, 0)
     for h in range(HOME):
         return_head(h, 1)
+    n_tokens = n_seq * BLOCK * n_dp
     gain_start(1, gain_finish(0))
-    gain_start(2, gain_finish(1))
-    n_tokens = n_seq * BLOCK * n_dp
-    gain_start(3, gain_finish(2) * (1.0 / math.sqrt(n_tokens)))
+    gain_start(2, gain_finish(1) * (1.0 / math.sqrt(n_tokens)))
 
     def await_returns(t):
         def step(h, carry):
@@ -353,9 +413,9 @@
         return store
 
     stores = [finish(0, dq_out), finish(1, dk_out)]
-    gain_finish(3)
-    for t in range(RING):
-        gain_out[t] = fin[t]
+    gain_finish(2)
+    stores.append(pltpu.make_async_copy(fin, gain_out, store_sem.at[2]))
+    stores[2].start()
     await_returns(1)
     for store in stores:
         store.wait()
@@ -369,33 +429,39 @@
                 forward(h, d, g).wait_send()
                 give_back(h, d, g).wait_send()
         for s in range(2):
-            halo(h, s).wait_send()
-            halo_back(h, s).wait_send()
+            sent_by(s, halo(h, s), "wait_send")
+            sent_by(s, halo_back(h, s), "wait_send")
         return carry
 
     lax.fori_loop(0, HOME, drain, 0)
-    for stage in range(4):
+    for stage in range(3):
         for d in range(1, gain_stages[stage][2]):
             gain_copy(stage, d, True).wait_send()
 
 
-def hand_over(dq_ref, dk_ref, dv_ref, gain_ref, dq_out, dk_out, dv_out, q_sum, k_sum, held, in_sem, out_sem):
-    loads = [
-        pltpu.make_async_copy(src, held.at[i], in_sem.at[i]) for i, src in enumerate((dq_ref, dk_ref, dv_ref))
-    ]
-    stores = [
-        pltpu.make_async_copy(held.at[i], dst, out_sem.at[i]) for i, dst in enumerate((dq_out, dk_out, dv_out))
-    ]
+def hand_over(
+    dq_ref, dk_ref, dv_ref, gain_ref, dq_out, dk_out, dv_out, q_out, k_out, held, gains, q_sum, k_sum, in_sem, out_sem
+):
+    def copy(src, dst, sem, i):
+        return pltpu.make_async_copy(src, dst, sem.at[i])
+
+    loads = [copy(gain_ref, gains, in_sem, 0)]
+    loads += [copy(src, held.at[i], in_sem, i + 1) for i, src in enumerate((dq_ref, dk_ref, dv_ref))]
+    stores = [copy(held.at[i], dst, out_sem, i) for i, dst in enumerate((dq_out, dk_out, dv_out))]
     for load in loads:
         load.start()
-    for load, store in zip(loads, stores):
-        load.wait()
-        store.start()
+    loads[0].wait()
     for home in range(RING):
         for h in range(HOME):
             cols = pl.ds((home * HOME + h) * HEAD_DIM, HEAD_DIM)
-            q_sum[cols] = gain_ref[home, h]
-            k_sum[cols] = gain_ref[home, 8 + h]
+            q_sum[cols] = gains[home, h]
+            k_sum[cols] = gains[home, 8 + h]
+    for load, store in zip(loads[1:], stores):
+        load.wait()
+        store.start()
+    stores += [copy(q_sum, q_out, out_sem, 3), copy(k_sum, k_out, out_sem, 4)]
+    for store in stores[3:]:
+        store.start()
     for store in stores:
         store.wait()
 
@@ -405,9 +471,8 @@
     flat = (BLOCK, WIDTH)
     half = jnp.bfloat16
     anywhere = pl.BlockSpec(memory_space=pl.ANY)
-    vmem = pl.BlockSpec(memory_space=pltpu.VMEM)
     dma = pltpu.SemaphoreType.DMA
-    n_gain = n_dp + n_x + n_z + RING
+    n_gain = n_dp * n_x + n_z + RING
     pair = (2, 2 * BLOCK, HEAD_DIM)
     d_q, d_k, d_v, gains = pl.pallas_call(
         functools.partial(kernel, sizes),
@@ -417,12 +482,14 @@
             jax.ShapeDtypeStruct(flat, half),
             jax.ShapeDtypeStruct((RING, 16, HEAD_DIM), jnp.float32),
         ),
-        in_specs=[anywhere] * 4 + [vmem, vmem, pl.BlockSpec(memory_space=pltpu.SMEM)],
-        out_specs=(anywhere, anywhere, anywhere, vmem),
+        in_specs=[anywhere] * 6 + [pl.BlockSpec(memory_space=pltpu.SMEM)],
+        out_specs=(anywhere,) * 4,
         scratch_shapes=[
             pltpu.VMEM((2,) + flat, half),
             pltpu.VMEM((4,) + flat, half),
             pltpu.VMEM((2, BLOCK, HEAD_DIM), jnp.float32),
+            pltpu.VMEM((WIDTH,), jnp.float32),
+            pltpu.VMEM((WIDTH,), jnp.float32),
             pltpu.VMEM((2, 1, WIDTH), jnp.float32),
             pltpu.VMEM((8, HEAD_DIM), jnp.float32),
             pltpu.VMEM((RING, 8, HEAD_DIM), jnp.float32),
@@ -434,10 +501,9 @@
             pltpu.VMEM((2,) + flat, half),
             pltpu.VMEM((RING, 16, HEAD_DIM), jnp.float32),
             pltpu.VMEM((16, HEAD_DIM), jnp.float32),
-            pltpu.VMEM((n_dp, 16, HEAD_DIM), jnp.float32),
-            pltpu.VMEM((n_x, 16, HEAD_DIM), jnp.float32),
+            pltpu.VMEM((n_dp * n_x, 16, HEAD_DIM), jnp.float32),
             pltpu.VMEM((n_z, 16, HEAD_DIM), jnp.float32),
-            dma((4,)),
+            dma((6,)),
             dma((HOME, RING, 2)),
             dma((HOME, RING, 2)),
             dma((RING,)),
@@ -450,7 +516,8 @@
             dma((HOME, RING, 2)),
             dma((n_gain,)),
             dma((n_gain,)),
-            dma((2,)),
+            pltpu.SemaphoreType.REGULAR((2, TOKENS)),
+            dma((3,)),
         ],
         compiler_params=pltpu.CompilerParams(
             collective_id=0, has_side_effects=True, vmem_limit_bytes=62 * 1024 * 1024
@@ -462,9 +529,16 @@
     out = pl.pallas_call(
         hand_over,
         out_shape=(jax.ShapeDtypeStruct(flat, half),) * 3 + (jax.ShapeDtypeStruct((WIDTH,), jnp.float32),) * 2,
-        in_specs=[anywhere] * 3 + [vmem],
-        out_specs=(anywhere,) * 3 + (vmem,) * 2,
-        scratch_shapes=[pltpu.VMEM((3,) + flat, half), dma((3,)), dma((3,))],
+        in_specs=[anywhere] * 4,
+        out_specs=(anywhere,) * 5,
+        scratch_shapes=[
+            pltpu.VMEM((3,) + flat, half),
+            pltpu.VMEM((RING, 16, HEAD_DIM), jnp.float32),
+            pltpu.VMEM((WIDTH,), jnp.float32),
+            pltpu.VMEM((WIDTH,), jnp.float32),
+            dma((4,)),
+            dma((5,)),
+        ],
     )(d_q, d_k, d_v, gains)
     shape = q_raw.shape
     return tuple(part.reshape(shape) for part in out[:3]) + out[3:]

time: 126 us -> 119 us (0.944)
  Pallas kernels: 125 us -> 117 us
    pallas_call x1, Pallas kernels: 121 us -> 115 us  [body(): pl.pallas_call(functools.partial(kernel, sizes), out_shape=(jax.ShapeDtyp...]
    pallas_call x1, Pallas kernels: 3.77 us -> 2.46 us  [body(): pl.pallas_call(hand_over, out_shape=(jax.ShapeDtypeStruct(flat, half),) *...]
where the time goes in v3:
time: 119 us; the launch traced here: 118 us
  Pallas kernels  117 us (98%)
    pallas_call x1, Pallas kernels, body(): pl.pallas_call(functools.partial(kernel, sizes), out_shape=(jax.ShapeDtyp...  115 us
    pallas_call x1, Pallas kernels, body(): pl.pallas_call(hand_over, out_shape=(jax.ShapeDtypeStruct(flat, half),) *...  2.46 us

profile of v3, /device:TPU:1, one launch (start us, length us, event | category | flops | bytes accessed | tf_op | source)
XLA Modules:
  0.0 118.0 jit_solution(818199867882574349)
XLA Ops:
  0.6 114.9 %shard_map.110 = (bf16[128,2560]{1,0:T(8,128)(2,1)}, bf16[128,2560]{1,0:T(8,128)(2,1)}, bf16[128,2560]{1,0:T(8,128)(2,1)}, f32[4,16,128]{2,1,0:T(8,128)}) custom-call(bf16[128,2560]{1,0:T(8,128)(2,1)} %bitcast.7, bf16[128,2560]{1,0:T(8,128)(2,1)} %bitcast.8, bf16[128,2560]{1,0:T(8,128)(2,1)} %bitcast.9, bf16[128,2560]{1,0:T(8,128)(2,1)} %bitcast.10, ...), custom_call_target="tpu_custom_call" | custom-call | tf_op jit(solution)/shard_map/pallas_call | solution.py:477
  115.6 2.5 %shard_map.111 = (bf16[128,2560]{1,0:T(8,128)(2,1)}, bf16[128,2560]{1,0:T(8,128)(2,1)}, bf16[128,2560]{1,0:T(8,128)(2,1)}, f32[2560]{0:T(1024)}, f32[2560]{0:T(1024)}) custom-call(bf16[128,2560]{1,0:T(8,128)(2,1)} %get-tuple-element.14.dq_ref, bf16[128,2560]{1,0:T(8,128)(2,1)} %get-tuple-element.15.dk_ref, bf16[128,2560]{1,0:T(8,128)(2,1)} %get-tuple-element.16.dv_ref, ...), custom_call_target="tpu_custom_call" | custom-call | tf_op jit(solution)/shard_map/pallas_call | solution.py:529
